TPU v7x, 256 devices: a whole 4x4x8 slice. The times are simulated.
256 devices in a mesh: dp: 32 (over x, y, core), mp: 8 (over z).
Axes of the slice: x: 4, y: 4, z: 8, core: 2. Of those that a mesh axis runs over, the one named last changes fastest.
Arguments:
- tokens: bfloat16 [32768, 4096], P(('dp', 'mp')), may hold values from -200 to 200
- w_query: bfloat16 [4096, 2048], P(None, 'mp'), may hold values from -0.09375 to 0.09375
- w_key: bfloat16 [896, 2048], P(None, 'mp'), may hold values from -0.1875 to 0.1875
- w_value: bfloat16 [896, 2048], P(None, 'mp'), may hold values from -0.1875 to 0.1875
- w_out: bfloat16 [2048, 4096], P('mp'), may hold values from -0.375 to 0.375
- encoded: bfloat16 [512, 128, 896], P('dp'), may hold values from -6 to 6
- nbr_shard: int32 [512, 2], P('dp'), may hold values from 0 to 31, as said below
- nbr_row: int32 [512, 2], P('dp'), may hold values from 0 to 15
Outputs:
- mixed: bfloat16 [32768, 4096], P(('dp', 'mp'))
Inputs may be any that keep to these rules, and one draw needn't show every extreme that they name: `nbr_shard`: the 32 neighbours of one sequence's spans name each cache shard either never or exactly 2 times; how often a shard is named over all sequences differs widely between shards.
All inputs are finite; a program needn't handle non-finite values.
Results may differ from a plain program's by a relative error of at most 0.019.
The roundings to bfloat16 on the way count: a program that leaves them out, or rounds other values in their place, can miss the bound.
Values may be sent and summed in bfloat16 or wider, within the bound.
A program may use at most 128 MiB of HBM per device.

v0:
```python
import math

import jax
import jax.numpy as jnp
from jax import lax
from jax.sharding import PartitionSpec as P

HD = 128
SPAN = 64
NLEN = 128
NBR = 2


def shifted_blocks(queries):
    row_width = queries.shape[1]
    zero_tail = jnp.zeros((SPAN - 1, row_width), queries.dtype)
    shifted = jnp.concatenate([queries[SPAN - 1 :], zero_tail], axis=0)
    return shifted.reshape(queries.shape[0] // SPAN, SPAN, row_width)


def attend_block(query_blocks, key_rows, value_rows):
    block_count = query_blocks.shape[0]
    head_count = query_blocks.shape[2] // HD
    query_heads = query_blocks.reshape(block_count, SPAN, head_count, HD)
    key_heads = key_rows.reshape(block_count, NLEN, head_count, HD)
    value_heads = value_rows.reshape(block_count, NLEN, head_count, HD)
    scores = jnp.einsum(
        "bqhd,bkhd->bhqk", query_heads, key_heads, preferred_element_type=jnp.float32
    ) * jnp.float32(1.0 / math.sqrt(HD))
    peak_score = jnp.max(scores, axis=3, keepdims=True)
    exponent = jnp.exp(scores - peak_score)
    totals = jnp.sum(exponent, axis=3, keepdims=True)
    weights = exponent.astype(jnp.bfloat16)
    summed = jnp.einsum("bhqk,bkhd->bqhd", weights, value_heads, preferred_element_type=jnp.float32)
    scaled = summed / jnp.transpose(totals, (0, 2, 1, 3))
    partial_value = scaled.astype(jnp.bfloat16).reshape(block_count, SPAN, head_count * HD)
    spread = (peak_score + jnp.log(totals))[..., 0]
    return (partial_value, spread)


def combine(partial_value, spread):
    span_count = partial_value.shape[0] // NBR
    head_count = spread.shape[1]
    spread = spread.reshape(span_count, NBR, head_count, SPAN)
    top_scale = jnp.max(spread, axis=1, keepdims=True)
    shares = jnp.exp(spread - top_scale)
    shares = shares / jnp.sum(shares, axis=1, keepdims=True)
    shares = jnp.transpose(shares, (0, 1, 3, 2))[..., None]
    pieces = (
        lax.optimization_barrier(partial_value)
        .astype(jnp.float32)
        .reshape(span_count, NBR, SPAN, head_count, HD)
    )
    merged = jnp.sum(pieces * shares, axis=1)
    return merged.astype(jnp.bfloat16).reshape(span_count * SPAN, head_count * HD)


def unshifted(attention):
    zero_head = jnp.zeros((SPAN - 1, attention.shape[1]), attention.dtype)
    return jnp.concatenate([zero_head, attention[: attention.shape[0] - (SPAN - 1)]], axis=0)


def shards(tokens, w_query, w_key, w_value, w_out, encoded, nbr_shard, nbr_row):
    queries = jnp.dot(
        lax.all_gather(tokens, "mp", axis=0, tiled=True),
        w_query,
        preferred_element_type=jnp.float32,
    ).astype(jnp.bfloat16)
    blocks = shifted_blocks(queries)
    head_width = w_query.shape[1]
    groups = lax.axis_size("dp")
    span_count = nbr_shard.shape[0]
    fetches = span_count * NBR
    capacity = NBR * ((span_count + groups - 1) // groups)
    shard_flat = nbr_shard.reshape(fetches)
    row_flat = nbr_row.reshape(fetches)
    fetch_ids = jnp.arange(fetches, dtype=jnp.int32)
    earlier = (shard_flat[:, None] == shard_flat[None, :]) & (
        fetch_ids[None, :] < fetch_ids[:, None]
    )
    slot_rank = jnp.sum(earlier.astype(jnp.int32), axis=1)
    slot_of = shard_flat * capacity + slot_rank
    slot_ids = jnp.arange(groups * capacity, dtype=jnp.int32)
    fetch_of_slot = (
        jnp.sum(jnp.where(slot_of[None, :] == slot_ids[:, None], fetch_ids[None, :] + 1, 0), axis=1)
        - 1
    )
    safe_fetch = jnp.maximum(fetch_of_slot, 0)
    asked_rows = jnp.where(fetch_of_slot >= 0, jnp.take(row_flat, safe_fetch), -1).reshape(
        groups, capacity
    )
    enc_width = encoded.shape[2]
    arrived = lax.all_to_all(
        jnp.take(
            encoded,
            jnp.maximum(
                lax.all_to_all(asked_rows, "dp", split_axis=0, concat_axis=0, tiled=True), 0
            ),
            axis=0,
        ),
        "dp",
        split_axis=0,
        concat_axis=0,
        tiled=True,
    )
    picked_rows = jnp.take(arrived.reshape(groups * capacity, NLEN, enc_width), slot_of, axis=0)
    flat_rows = picked_rows.reshape(fetches * NLEN, enc_width)
    key_rows = (
        jnp.dot(flat_rows, w_key, preferred_element_type=jnp.float32)
        .astype(jnp.bfloat16)
        .reshape(fetches, NLEN, head_width)
    )
    value_rows = (
        jnp.dot(flat_rows, w_value, preferred_element_type=jnp.float32)
        .astype(jnp.bfloat16)
        .reshape(fetches, NLEN, head_width)
    )
    partial_value, spread = attend_block(jnp.repeat(blocks, NBR, axis=0), key_rows, value_rows)
    attended = unshifted(combine(partial_value, spread))
    return lax.psum_scatter(
        jnp.dot(attended, w_out, preferred_element_type=jnp.float32).astype(jnp.bfloat16),
        "mp",
        scatter_dimension=0,
        tiled=True,
    )


def solution(mesh):
    return jax.shard_map(
        shards,
        mesh=mesh,
        in_specs=(
            P(("dp", "mp"), None),
            P(None, "mp"),
            P(None, "mp"),
            P(None, "mp"),
            P("mp", None),
            P("dp", None, None),
            P("dp", None),
            P("dp", None),
        ),
        out_specs=P(("dp", "mp"), None),
        check_vma=False,
    )
```

profile of v0, /device:TPU:1, one launch (start us, length us, event | category | flops | bytes accessed | tf_op | source)
XLA Modules:
  0.0 461.2 jit_solution(1835139292508420486)
XLA Ops:
  6.5 0.0 copy-start
  6.5 0.9 copy.38
  7.4 0.1 reshape.177
  7.5 0.2 convert_reduce_fusion
  7.7 0.1 select_reduce_fusion
  7.9 0.8 copy.39
  8.6 0.1 reshape.178
  8.7 0.8 gather_fusion
  9.5 0.1 reshape.185
  9.6 15.3 %all_to_all.11 = s32[32,1,2]{2,1,0:T(1,128)S(1)} all-to-all(s32[32,1,2]{2,1,0:T(1,128)S(1)} %bitcast.62), channel_id=1, replica_groups=mesh['dp'=32,'mp'=8] {'dp'}, dimensions={0} | all-to-all | bytes 512 | tf_op jit(solution)/shard_map/all_to_all | solution.py:97
  24.9 0.1 maximum_reduce_fusion
  25.0 0.1 reshape.198
  25.1 0.1 copy.41
  25.2 0.1 copy.42
  25.3 10.0 %gather_fusion.1 = bf16[64,128,896]{2,1,0:T(8,128)(2,1)} fusion(bf16[16,128,896]{2,1,0:T(8,128)(2,1)} %param.13, s32[1024]{0:T(1024)S(1)} %pad_clamp_fusion.1), kind=kCustom, calls=%fused_computation.1 | custom fusion | bytes 29360384 | tf_op jit(solution)/shard_map/jit(_take)/gather | solution.py:94
  35.4 13.7 %broadcast_select_fusion = bf16[32,2,128,896]{3,2,1,0:T(8,128)(2,1)} fusion(bf16[32,2,128,896]{3,2,1,0:T(8,128)(2,1)} %bitcast.56, pred[32,2]{1,0:T(8,128)(4,1)S(1)} %copy.42), kind=kLoop, calls=%fused_computation.3 | loop fusion | flops 7340032 | bytes 29360192 | tf_op jit(solution)/shard_map/jit(_take)/select_n | solution.py:94
  49.0 0.0 copy-start.3
  49.0 5.9 %all-to-all-start.1 = ((bf16[32,2,128,896]{3,2,1,0:T(8,128)(2,1)}), bf16[32,2,128,896]{3,2,1,0:T(8,128)(2,1)}, u32[]{:S(2)}, u32[]{:S(2)}) async-start(bf16[32,2,128,896]{3,2,1,0:T(8,128)(2,1)} %broadcast_select_fusion), calls=%async_computation.1 | async-start | bytes 29360128 | tf_op jit(solution)/shard_map/all_to_all | solution.py:93
  54.9 0.0 all-gather.2.cloned.1.call-start
  54.9 0.7 all-gather.2.cloned.1.call-update
  55.6 0.0 reduce-scatter.2.cloned.1.call-start
  55.7 0.0 copy-done.3
  55.7 0.1 copy.43
  55.8 0.1 mul.44
  55.9 0.1 broadcast_bitcast_fusion
  56.0 200.8 %all-to-all-done.1 = bf16[32,2,128,896]{3,2,1,0:T(8,128)(2,1)} async-done(((bf16[32,2,128,896]{3,2,1,0:T(8,128)(2,1)}), bf16[32,2,128,896]{3,2,1,0:T(8,128)(2,1)}, u32[]{:S(2)}, u32[]{:S(2)}) %all-to-all-start.1) | async-done | bytes 14680096 | tf_op jit(solution)/shard_map/all_to_all | solution.py:93
  256.8 9.5 %gather_fusion.2 = bf16[32,128,896]{2,1,0:T(8,128)(2,1)} fusion(bf16[64,128,896]{2,1,0:T(8,128)(2,1)} %bitcast.4, s32[1024]{0:T(1024)S(1)} %pad_clamp_fusion), kind=kCustom, calls=%fused_computation.2 | custom fusion | bytes 14680192 | tf_op jit(solution)/shard_map/jit(_take)/gather | solution.py:106
  266.3 0.0 copy-start.4
  266.3 4.3 bitcast_select_fusion
  270.6 0.0 copy-start.2
  270.6 3.0 copy-done.2
  273.6 0.0 copy-done.4
  273.6 3.7 convolution_convert_fusion.1
  277.3 0.0 copy-start.5
  277.3 4.1 reshape_reshape.11
  281.3 0.0 copy-done.5
  281.3 6.7 %convolution_convert_fusion.2 = bf16[4096,256]{1,0:T(8,128)(2,1)} fusion(bf16[4096,896]{1,0:T(8,128)(2,1)} %copy-done.2, bf16[896,256]{1,0:T(8,128)(2,1)S(1)} %copy-done.5), kind=kOutput, calls=%fused_computation.7 | convolution fusion | flops 1880096768 | bytes 9895936 | tf_op jit(solution)/shard_map/dot_general | solution.py:114
  288.1 4.0 reshape_reshape.9
  292.1 0.0 all-gather.2.cloned.1.call-done
  292.1 6.3 %fusion.23 = bf16[1024,256]{1,0:T(8,128)(2,1)S(1)} fusion(bf16[1024,4096]{1,0:T(8,128)(2,1)} %all-gather.2.cloned.1.call-done, bf16[4096,256]{1,0:T(8,128)(2,1)} %param.9), kind=kOutput, calls=%fused_computation.57 | convolution fusion | flops 2147483648 | bytes 11010048 | tf_op jit(solution)/shard_map/dot_general | solution.py:64
  298.4 0.1 slice.17
  298.5 1.1 broadcast_in_dim.68
  299.6 1.3 reshape_reshape.10
  301.0 3.2 multiply_reduce_fusion.1
  304.2 0.0 copy-start.1
  304.2 1.3 copy-done.1
  305.5 1.4 fusion.5
  307.0 0.1 fusion.18
  307.0 0.1 divide_bitcast_fusion
  307.1 0.4 copy.48
  307.5 3.4 fusion.9
  310.9 1.2 copy.67
  312.1 3.1 reshape.187
  315.2 4.8 %multiply_reduce_fusion = bf16[16,64,2,128]{3,2,1,0:T(2,128)(2,1)S(1)} fusion(f32[16,2,64,2,128]{4,3,2,1,0:T(2,128)} %reshape.187, f32[16,2,64,2]{3,2,1,0:T(8,128)S(1)} %copy.48), kind=kLoop, calls=%fused_computation.14 | loop fusion | flops 786432 | bytes 2637824 | tf_op jit(solution)/shard_map/reduce_sum | solution.py:54
  320.0 0.1 copy.68
  320.2 0.0 copy-done
  320.2 5.6 %convolution_convert_fusion = bf16[1024,4096]{1,0:T(8,128)(2,1)} fusion(bf16[256,4096]{1,0:T(8,128)(2,1)S(1)} %copy-done, bf16[961,256]{1,0:T(8,128)(2,1)S(1)} %slice.15), kind=kOutput, calls=%fused_computation.4 | convolution fusion | flops 2151677952 | bytes 10977792 | tf_op jit(solution)/shard_map/dot_general | solution.py:121
  325.8 0.0 reduce-scatter.2.cloned.1.call-update
  325.8 128.5 %reduce-scatter.2.cloned.1.call-done = bf16[128,4096]{1,0:T(8,128)(2,1)} async-done(((bf16[1024,4096]{1,0:T(8,128)(2,1)}), bf16[128,4096]{1,0:T(8,128)(2,1)}) %reduce-scatter.2.cloned.1.call-update) | async-done | bytes 1048592 | tf_op jit(solution)/shard_map/reduce_scatter | solution.py:120
  (13 shorter events, 0.2 us)
Async XLA Ops:
  6.5 313.6 %copy-start = (bf16[256,4096]{1,0:T(8,128)(2,1)S(1)}, bf16[256,4096]{1,0:T(8,128)(2,1)}, u32[]{:S(2)}) copy-start(bf16[256,4096]{1,0:T(8,128)(2,1)} %param.12) | copy-start | bytes 6291460
  49.0 6.7 %copy-start.3 = (s32[16,2]{0,1:T(2,128)S(1)}, s32[16,2]{0,1:T(2,128)}, u32[]{:S(2)}) copy-start(s32[16,2]{0,1:T(2,128)} %param.14) | copy-start | bytes 388
  49.0 207.8 %all-to-all-start.1 = ((bf16[32,2,128,896]{3,2,1,0:T(8,128)(2,1)}), bf16[32,2,128,896]{3,2,1,0:T(8,128)(2,1)}, u32[]{:S(2)}, u32[]{:S(2)}) async-start(bf16[32,2,128,896]{3,2,1,0:T(8,128)(2,1)} %broadcast_select_fusion), calls=%async_computation.1 | async-start | bytes 29360128 | tf_op jit(solution)/shard_map/all_to_all | solution.py:93
  54.9 237.2 %all-gather.2.cloned.1.call-start = ((), (), s32[]{:S(2)}) async-start(), calls=%async_computation.3 | async-start | bytes 9437184 | tf_op jit(solution)/shard_map/all_gather | solution.py:65
  55.6 398.7 %reduce-scatter.2.cloned.1.call-start = ((), (), s32[]{:S(2)}) async-start(), calls=%async_computation.4 | async-start | bytes 9437184 | tf_op jit(solution)/shard_map/reduce_scatter | solution.py:120
  266.3 7.3 %copy-start.4 = (bf16[896,256]{1,0:T(8,128)(2,1)S(1)}, bf16[896,256]{1,0:T(8,128)(2,1)}, u32[]{:S(2)}) copy-start(bf16[896,256]{1,0:T(8,128)(2,1)} %param.10) | copy-start | bytes 1376260
  270.6 3.0 copy-start.2
  277.3 4.1 copy-start.5
  304.2 1.3 copy-start.1
Sparse Core Ops, SparseCore 0:
  57.5 96.8 all-gather.1
  325.9 128.3 reduce-scatter.1
where the time goes:
time: 462 us; the launch traced here: 461 us
  waiting for transfers between devices  330 us (71%)
  local copies, waits for them, and re-layouts  42.5 us (9%)
  matrix products  29 us (6%)
  other arithmetic  24.8 us (5%)
  blocking collectives  15.3 us (3%)
  between operations  13.6 us (3%)
  starting transfers between devices  5.94 us (1%)
    all_to_all x1, waiting for transfers between devices, shards(): lax.all_to_all(jnp.take(encoded, jnp.maximum(lax.all_to_all(asked_rows, '...  201 us
    reduce_scatter x1, waiting for transfers between devices, shards(): lax.psum_scatter(jnp.dot(attended, w_out, preferred_element_type=jnp.floa...  129 us
    all_to_all x1, blocking collectives, shards(): lax.all_to_all(asked_rows, 'dp', split_axis=0, concat_axis=0, tiled=True)  15.3 us
    select_n x1, other arithmetic, shards(): jnp.take(encoded, jnp.maximum(lax.all_to_all(asked_rows, 'dp', split_axis...  13.7 us
    gather x1, local copies, waits for them, and re-layouts, shards(): jnp.take(encoded, jnp.maximum(lax.all_to_all(asked_rows, 'dp', split_axis...  10 us
    gather x1, local copies, waits for them, and re-layouts, shards(): jnp.take(arrived.reshape(groups * capacity, NLEN, enc_width), slot_of, ax...  9.5 us
  transfers between devices with their start and end apart: 3, of which 2 were waited for; matrix products, arithmetic and copies ran while one was open for 7% of the time, Pallas kernels for 0%

commit v1 on v0

v1 whole, which is shorter than its diff:
```python
import functools
import math

import jax
import jax.numpy as jnp
from jax import lax
from jax.experimental import pallas as pl
from jax.experimental.pallas import tpu as pltpu
from jax.sharding import PartitionSpec as P

MESH = pl.DeviceIdType.MESH
BF = jnp.bfloat16
F32 = jnp.float32
HD = 128
SPAN = 64
D = 4096
ENC = 896
TOK = 128
NX = 4
NZ = 8
NP = 32
ROWS = 16
QZ = 1024
QU = (D - QZ) // 16
OU = D // 16
SLOTS = ((1, 0), (1, 1), (2, 0), (2, 1), (3, 0), (3, 1), (0, 1))
OUT_CHUNK = 512


def kernel(
    tok, wq, wk, wv, wo, enc, ask, slot, out,
    tokv, ttail, wqb, wkb, wvb, wob, band, ask_r, ask_s, send_e, recv_e, send_z, encz,
    qb, kb, vb, att, att0, acc, t_send, t_recv, r_own, r_in,
    l_sem, sz, rz, sx, rx, sa, ra, se, re, s2, r2, st, rt, sf, rf,
):
    d = lax.axis_index("dp")
    z = lax.axis_index("mp")
    x = d // 8
    y = lax.rem(d // 2, 4)
    c = lax.rem(d, 2)
    other = (d + 1 - 2 * c, z)
    zdn = (d, lax.rem(z + 7, NZ))
    zup = (d, lax.rem(z + 1, NZ))
    odn = (other[0], zdn[1])
    oup = (other[0], zup[1])

    def plane(px, py):
        return (px * 8 + py * 2 + c, z)

    ring = {
        "x": (plane(lax.rem(x + 1, 4), y), plane(lax.rem(x + 3, 4), y)),
        "y": (plane(x, lax.rem(y + 1, 4)), plane(x, lax.rem(y + 3, 4))),
    }
    cs = pl.ds(pl.multiple_of(c * HD, HD), HD)

    def remote(src, dst, ssem, rsem, dev):
        return pltpu.make_async_remote_copy(
            src_ref=src, dst_ref=dst, send_sem=ssem, recv_sem=rsem, device_id=dev, device_id_type=MESH
        )

    half0 = pl.ds(0, HD)
    local = [
        pltpu.make_async_copy(enc.at[:, pl.ds(pl.multiple_of(z * ROWS, ROWS), ROWS), :], band, l_sem.at[0]),
        pltpu.make_async_copy(tok, tokv.at[pl.ds(0, TOK)], l_sem.at[1]),
        pltpu.make_async_copy(wq.at[:, cs], wqb.at[0, :, half0], l_sem.at[2]),
        pltpu.make_async_copy(wk.at[:, cs], wkb.at[0, :, half0], l_sem.at[3]),
        pltpu.make_async_copy(wv.at[:, cs], wvb.at[0, :, half0], l_sem.at[4]),
        pltpu.make_async_copy(wo.at[cs, :], wob.at[0, half0, :], l_sem.at[5]),
    ]
    for copy in local:
        copy.start()

    bar = pltpu.get_barrier_semaphore()

    def greet_plane(k, carry):
        pl.semaphore_signal(bar, inc=1, device_id=(lax.rem(d + k, NP), z), device_id_type=MESH)
        return carry

    def greet_z(k, carry):
        pl.semaphore_signal(bar, inc=1, device_id=(d, lax.rem(z + k, NZ)), device_id_type=MESH)
        return carry

    lax.fori_loop(1, NP, greet_plane, 0)
    lax.fori_loop(1, NZ, greet_z, 0)
    pl.semaphore_signal(bar, inc=1, device_id=odn, device_id_type=MESH)
    pl.semaphore_signal(bar, inc=1, device_id=oup, device_id_type=MESH)
    pl.semaphore_wait(bar, NP - 1 + NZ - 1 + 2)

    qi = y * 4 + x
    oi = x * 4 + y

    def q_at(sl, start, size):
        if sl is None:
            return wq.at[pl.ds(start, size), cs]
        return wqb.at[sl[0], pl.ds(start, size), pl.ds(sl[1] * HD, HD)]

    def o_at(sl, start, size):
        if sl is None:
            return wo.at[cs, pl.ds(start, size)]
        return wob.at[sl[0], pl.ds(sl[1] * HD, HD), pl.ds(start, size)]

    def kv_at(arg, buf, sl):
        if sl is None:
            return arg.at[:, cs]
        return buf.at[sl[0], :, pl.ds(sl[1] * HD, HD)]

    started = []

    def go(copy):
        copy.start()
        started.append(copy)
        return copy

    def flush(keep):
        while len(started) > keep:
            started.pop(0).wait_send()

    zc = {}

    def z_copy(way, k, part):
        src_sl = None if k == 1 else (k - 1, way)
        dst_sl = (k, way) if k < 4 else (0, 1)
        if part == 0:
            start = pl.multiple_of(QZ + qi * QU + (QU // 2 if k == 4 and way else 0), 16)
            size = QU // 2 if k == 4 else QU
            src, dst = q_at(src_sl, start, size), q_at(dst_sl, start, size)
        elif part == 1:
            start = pl.multiple_of(oi * OU + (OU // 2 if k == 4 and way else 0), 128)
            size = OU // 2 if k == 4 else OU
            src, dst = o_at(src_sl, start, size), o_at(dst_sl, start, size)
        elif part == 2:
            src, dst = kv_at(wk, wkb, src_sl), kv_at(wk, wkb, dst_sl)
        elif part == 3:
            src, dst = kv_at(wv, wvb, src_sl), kv_at(wv, wvb, dst_sl)
        else:
            start = QZ // 2 if k == 4 and way else 0
            size = QZ // 2 if k == 4 else QZ
            src, dst = q_at(src_sl, start, size), q_at(dst_sl, start, size)
        zc[way, k, part] = go(
            remote(src, dst, sz.at[way, k - 1, part], rz.at[way, k - 1, part], zup if way else zdn)
        )

    def z_parts(way, k, parts):
        return [p for p in parts if not (k == 4 and p == (2 if way else 3))]

    def z_start(k, parts):
        for p in parts:
            for way in (0, 1):
                if p in z_parts(way, k, parts):
                    z_copy(way, k, p)

    def z_wait(k, parts):
        for p in parts:
            for way in (0, 1):
                if p in z_parts(way, k, parts):
                    zc[way, k, p].wait_recv()

    SL, BULK = (0, 1), (2, 3, 4)

    xc = {}

    def view(arr, sl, start, size):
        if arr == 0:
            return q_at(sl, pl.multiple_of(QZ + start, 16), size)
        return o_at(sl, pl.multiple_of(start, 128), size)

    unit = (QU, OU)
    first = (x, y)
    second = (y, x)
    axes = (("x", "y"), ("y", "x"))

    def x_start(t, phase):
        sl = SLOTS[t]
        for arr in (0, 1):
            u, i1, i2 = unit[arr], first[arr], second[arr]
            up, dn = ring[axes[arr][phase // 2]]
            if phase == 0:
                spans = [((i2 * 4 + i1) * u, u)] * 2
            elif phase == 1:
                spans = [
                    ((i2 * 4 + lax.rem(i1 + 3, 4)) * u, u // 2),
                    ((i2 * 4 + lax.rem(i1 + 1, 4)) * u + u // 2, u // 2),
                ]
            elif phase == 2:
                spans = [(i2 * 4 * u, 4 * u)] * 2
            else:
                spans = [
                    (lax.rem(i2 + 3, 4) * 4 * u, 2 * u),
                    (lax.rem(i2 + 1, 4) * 4 * u + 2 * u, 2 * u),
                ]
            for way, dev in enumerate((up, dn)):
                ref = view(arr, sl, *spans[way])
                xc[t, phase, arr, way] = go(
                    remote(ref, ref, sx.at[arr, t, phase * 2 + way], rx.at[arr, t, phase * 2 + way], dev)
                )

    def x_wait(t, phase):
        for arr in (0, 1):
            for way in (0, 1):
                xc[t, phase, arr, way].wait_recv()

    def step(t, phase):
        x_wait(t, phase)
        if phase < 3:
            x_start(t, phase + 1)

    z_start(1, SL)
    last16 = pl.ds(TOK - 16, 16)
    tail_in = go(remote(tok.at[last16], ttail, st.at[0], rt.at[0], zup))

    def ask_copy(k):
        p = lax.rem(d + k, NP)
        return remote(ask.at[p], ask_r.at[d], sa.at[k], ra.at[k], (p, z))

    def each(n, f):
        def body(k, carry):
            f(k)
            return carry

        lax.fori_loop(1, n, body, 0)

    each(NP, lambda k: ask_copy(k).start())
    z_start(1, BULK)
    ask_r[pl.ds(d, 1)] = ask[pl.ds(d, 1)]
    each(NP, lambda k: ask_copy(k).wait_recv())
    to_smem = pltpu.make_async_copy(ask_r, ask_s, l_sem.at[6])
    to_smem.start()
    to_smem.wait()
    local[0].wait()

    def pick(s, carry):
        for j in range(2):
            send_e[s, j] = band[ask_s[s, 0, j]]
        return carry

    lax.fori_loop(0, NP, pick, 0)

    def e1_copy(k):
        p = lax.rem(d + k, NP)
        return remote(send_e.at[p], recv_e.at[pl.ds(2 * d, 2)], se.at[k], re.at[k], (p, z))

    each(NP, lambda k: e1_copy(k).start())
    recv_e[pl.ds(2 * d, 2)] = send_e[d]

    local[1].wait()
    tail_in.wait_recv()
    is15 = lax.broadcasted_iota(jnp.int32, (16, D), 0) == 15
    tokv[TOK - 16 : TOK, :] = jnp.where(is15, ttail[...], tokv[TOK - 16 : TOK, :])
    tok_x = go(remote(tokv.at[pl.ds(0, TOK)], tokv.at[pl.ds(TOK, TOK)], st.at[1], rt.at[1], other))

    for k in range(1, 5):
        z_wait(k, SL)
        if k < 4:
            z_start(k + 1, SL)
            x_start(2 * k - 2, 0)
            x_start(2 * k - 1, 0)
        else:
            x_start(6, 0)

    def project(pair, half):
        lanes = pl.ds(0, 256) if half is None else pl.ds(half * HD, HD)
        width = 256 if half is None else HD

        def body(k, total):
            start = pl.multiple_of(k * 512, 512)
            return total + jnp.dot(
                tokv[:, pl.ds(start, 512)], wqb[pair, pl.ds(start, 512), lanes], preferred_element_type=F32
            )

        total = lax.fori_loop(0, D // 512, body, jnp.zeros((2 * TOK, width), F32))
        qb[:, lanes] = total.astype(BF)

    def keys_values(pair, half):
        lanes = pl.ds(0, 256) if half is None else pl.ds(half * HD, HD)

        def body(u, carry):
            rows = encz[pl.ds(2 * u, 2)].reshape(256, ENC)
            kb[u, :, lanes] = jnp.dot(rows, wkb[pair, :, lanes], preferred_element_type=F32).astype(BF)
            vb[u, :, lanes] = jnp.dot(rows, wvb[pair, :, lanes], preferred_element_type=F32).astype(BF)
            return carry

        lax.fori_loop(0, 4, body, 0)

    row_id = lax.broadcasted_iota(jnp.int32, (TOK, 256), 0)
    in_b = jnp.logical_and(row_id >= SPAN - 1, row_id < TOK - 1)
    blank = jnp.logical_and(lax.broadcasted_iota(jnp.int32, (TOK, HD), 0) < SPAN - 1, z == 0)

    def attend(half, dst):
        halves = (0, 1) if half is None else (half,)
        for s in range(2):
            for h in halves:
                lanes = pl.ds(h * HD, HD)
                q = qb[s * TOK : (s + 1) * TOK, lanes]
                ka, kb_ = kb[2 * s, :, lanes], kb[2 * s + 1, :, lanes]
                dims = (((1,), (1,)), ((), ()))
                sa_ = lax.dot_general(q, ka, dims, preferred_element_type=F32)
                sb_ = lax.dot_general(q, kb_, dims, preferred_element_type=F32)
                scores = jnp.where(in_b, sb_, sa_) * F32(1.0 / math.sqrt(HD))
                peak = jnp.max(scores, axis=1, keepdims=True)
                e = jnp.exp(scores - peak)
                total = jnp.sum(e, axis=1, keepdims=True)
                wa = jnp.where(in_b, 0.0, e).astype(BF)
                wb = jnp.where(in_b, e, 0.0).astype(BF)
                o = jnp.dot(wa, vb[2 * s, :, lanes], preferred_element_type=F32)
                o = o + jnp.dot(wb, vb[2 * s + 1, :, lanes], preferred_element_type=F32)
                o = jnp.where(blank, 0.0, o / total)
                dst[s * TOK : (s + 1) * TOK, lanes] = o.astype(BF)

    def add_out(pair, is_first):
        def body(k, carry):
            cols = pl.ds(pl.multiple_of(k * OUT_CHUNK, OUT_CHUNK), OUT_CHUNK)
            term = jnp.dot(att[...], wob[pair, :, cols], preferred_element_type=F32)
            acc[:, cols] = term if is_first else acc[:, cols] + term
            return carry

        lax.fori_loop(0, D // OUT_CHUNK, body, 0)

    step(0, 0)
    step(1, 0)
    step(0, 1)
    step(1, 1)
    tok_x.wait_recv()
    local[2].wait()
    project(0, 0)
    step(2, 0)
    step(3, 0)
    each(NP, lambda k: e1_copy(k).wait_recv())

    def pick_z(mz, carry):
        fa = lax.rem(4 * mz + 30, 32)
        for i in range(2):
            send_z[mz, i] = recv_e[slot[0, fa + i]]
            send_z[mz, 2 + i] = recv_e[slot[0, 4 * mz + i]]
        return carry

    lax.fori_loop(0, NZ, pick_z, 0)
    my_rows = pl.ds(pl.multiple_of(z * ROWS, ROWS), ROWS)

    def e2_copy(k):
        p = lax.rem(z + k, NZ)
        return remote(send_z.at[p], encz.at[pl.ds(0, 4), my_rows, :], s2.at[k], r2.at[k], (d, p))

    each(NZ, lambda k: e2_copy(k).start())
    encz[pl.ds(0, 4), my_rows, :] = send_z[z]
    step(0, 2)
    step(1, 2)
    step(2, 1)
    step(3, 1)
    z_wait(1, BULK)
    z_start(2, BULK)
    step(4, 0)
    step(5, 0)
    step(6, 0)
    each(NZ, lambda k: e2_copy(k).wait_recv())
    enc_x = go(remote(encz.at[pl.ds(0, 4)], encz.at[pl.ds(4, 4)], st.at[2], rt.at[2], other))
    flush(40)
    local[3].wait()
    local[4].wait()
    local[5].wait()
    enc_x.wait_recv()
    keys_values(0, 0)
    attend(0, att0)
    step(0, 3)
    step(1, 3)
    step(2, 2)
    step(3, 2)
    step(4, 1)
    step(5, 1)
    project(1, None)
    keys_values(1, None)
    z_wait(2, BULK)
    z_start(3, BULK)
    attend(None, att)
    add_out(1, True)
    flush(30)
    step(2, 3)
    step(3, 3)
    step(4, 2)
    step(5, 2)
    step(6, 1)
    project(2, None)
    keys_values(2, None)
    z_wait(3, BULK)
    z_start(4, BULK)
    attend(None, att)
    add_out(2, False)
    flush(30)
    step(4, 3)
    step(5, 3)
    step(6, 2)
    project(3, None)
    keys_values(3, None)
    attend(None, att)
    add_out(3, False)
    each(NP, lambda k: ask_copy(k).wait_send())
    each(NP, lambda k: e1_copy(k).wait_send())
    each(NZ, lambda k: e2_copy(k).wait_send())
    flush(4)
    step(6, 3)
    z_wait(4, BULK)
    project(0, 1)
    keys_values(0, 1)
    attend(1, att0)
    flush(0)

    def t_copy(k):
        cols = pl.ds(pl.multiple_of(k * OUT_CHUNK, OUT_CHUNK), OUT_CHUNK)
        return remote(t_send.at[:, cols], t_recv.at[:, cols], sf.at[k], rf.at[k], other)

    def last(k, carry):
        cols = pl.ds(pl.multiple_of(k * OUT_CHUNK, OUT_CHUNK), OUT_CHUNK)
        term = acc[:, cols] + jnp.dot(att0[...], wob[0, :, cols], preferred_element_type=F32)
        acc[0:TOK, cols] = term[:TOK]
        t_send[:, cols] = term[TOK:].astype(BF)
        r_own[:, cols] = term[TOK - 16 : TOK].astype(BF)
        t_copy(k).start()
        return carry

    n = D // OUT_CHUNK
    lax.fori_loop(0, n, last, 0)
    row_a = remote(r_own, r_in.at[0], sf.at[n], rf.at[n], zdn)
    row_b = remote(t_send.at[last16], r_in.at[1], sf.at[n + 1], rf.at[n + 1], odn)
    row_a.start()
    row_b.start()

    def finish(k, carry):
        cols = pl.ds(pl.multiple_of(k * OUT_CHUNK, OUT_CHUNK), OUT_CHUNK)
        t_copy(k).wait()
        out[:, cols] = (acc[0:TOK, cols] + t_recv[:, cols].astype(F32)).astype(BF)
        return carry

    lax.fori_loop(0, n, finish, 0)
    row_a.wait()
    row_b.wait()
    fixed = (r_in[0].astype(F32) + r_in[1].astype(F32)).astype(BF)
    out[TOK - 16 : TOK, :] = jnp.where(is15, fixed, out[TOK - 16 : TOK, :])


def fused(tokens, w_query, w_key, w_value, w_out, encoded, ask, slot):
    any_ = pl.BlockSpec(memory_space=pl.ANY)
    vmem = pl.BlockSpec(memory_space=pltpu.VMEM)
    smem = pl.BlockSpec(memory_space=pltpu.SMEM)
    dma = pltpu.SemaphoreType.DMA
    V = pltpu.VMEM
    n = D // OUT_CHUNK
    return pl.pallas_call(
        kernel,
        out_shape=jax.ShapeDtypeStruct((TOK, D), BF),
        in_specs=[any_] * 6 + [vmem, smem],
        out_specs=vmem,
        scratch_shapes=[
            V((2 * TOK, D), BF),
            V((16, D), BF),
            V((4, D, 256), BF),
            V((4, ENC, 256), BF),
            V((4, ENC, 256), BF),
            V((4, 256, D), BF),
            V((16, ROWS, ENC), BF),
            V((NP, 1, 128), jnp.int32),
            pltpu.SMEM((NP, 1, 128), jnp.int32),
            V((NP, 2, ROWS, ENC), BF),
            V((2 * NP, ROWS, ENC), BF),
            V((NZ, 4, ROWS, ENC), BF),
            V((8, 128, ENC), BF),
            V((2 * TOK, 256), BF),
            V((4, 256, 256), BF),
            V((4, 256, 256), BF),
            V((2 * TOK, 256), BF),
            V((2 * TOK, 256), BF),
            V((2 * TOK, D), F32),
            V((TOK, D), BF),
            V((TOK, D), BF),
            V((16, D), BF),
            V((2, 16, D), BF),
            dma((7,)),
            dma((2, 4, 5)),
            dma((2, 4, 5)),
            dma((2, 7, 8)),
            dma((2, 7, 8)),
            dma((NP,)),
            dma((NP,)),
            dma((NP,)),
            dma((NP,)),
            dma((NZ,)),
            dma((NZ,)),
            dma((3,)),
            dma((3,)),
            dma((n + 2,)),
            dma((n + 2,)),
        ],
        compiler_params=pltpu.CompilerParams(
            collective_id=0, has_side_effects=True, vmem_limit_bytes=56 * 1024 * 1024
        ),
    )(tokens, w_query, w_key, w_value, w_out, encoded, ask, slot)


def shards(tokens, w_query, w_key, w_value, w_out, encoded, nbr_shard, nbr_row):
    shard = nbr_shard.reshape(32)
    row = nbr_row.reshape(32)
    ids = jnp.arange(32, dtype=jnp.int32)
    earlier = (shard[:, None] == shard[None, :]) & (ids[None, :] < ids[:, None])
    slot = shard * 2 + jnp.sum(earlier.astype(jnp.int32), axis=1)
    lane = jnp.arange(128, dtype=jnp.int32)
    want = jnp.where(lane < 2, 2 * jnp.arange(NP, dtype=jnp.int32)[:, None] + lane[None, :], -1)
    ask = jnp.sum(jnp.where(slot[None, None, :] == want[:, :, None], row[None, None, :], 0), axis=2)
    return fused(
        tokens, w_query, w_key, w_value, w_out, encoded, ask.reshape(NP, 1, 128), slot.reshape(1, 32)
    )


def solution(mesh):
    return jax.shard_map(
        shards,
        mesh=mesh,
        in_specs=(
            P(("dp", "mp"), None),
            P(None, "mp"),
            P(None, "mp"),
            P(None, "mp"),
            P("mp", None),
            P("dp", None, None),
            P("dp", None),
            P("dp", None),
        ),
        out_specs=P(("dp", "mp"), None),
        check_vma=False,
    )
```

time: 462 us -> 148 us (0.32)
  waiting for transfers between devices: 330 us -> 0 us
  Pallas kernels: 0 us -> 141 us
  local copies, waits for them, and re-layouts: 42.5 us -> 4.15 us
  matrix products: 29 us -> 0 us
  other arithmetic: 24.8 us -> 2.3 us
  blocking collectives: 15.3 us -> 0 us
  between operations: 13.6 us -> 0.02 us
  starting transfers between devices: 5.94 us -> 0 us
    all_to_all x1 -> x0, waiting for transfers between devices: 201 us -> none  [shards(): lax.all_to_all(jnp.take(encoded, jnp.maximum(lax.all_to_all(asked_rows, '...]
    pallas_call x0 -> x1, Pallas kernels: none -> 141 us  [fused(): pl.pallas_call(kernel, out_shape=jax.ShapeDtypeStruct((TOK, D), BF), in_s...]
    reduce_scatter x1 -> x0, waiting for transfers between devices: 129 us -> none  [shards(): lax.psum_scatter(jnp.dot(attended, w_out, preferred_element_type=jnp.floa...]
    dot_general x6 -> x0, matrix products: 29 us -> none  [the longest x1 6.74 us: shards(): jnp.dot(flat_rows, w_value, preferred_element_type=jnp.float32)]
    gather x3 -> x0, local copies, waits for them, and re-layouts: 20.3 us -> none  [the longest x1 10 us: shards(): jnp.take(encoded, jnp.maximum(lax.all_to_all(asked_rows, 'dp', split_axis...]
    select_n x4 -> x1, other arithmetic: 18 us -> 0.07 us  [shards(): jnp.where(lane < 2, 2 * jnp.arange(NP, dtype=jnp.int32)[:, None] + lane[N...]
    all_to_all x1 -> x0, blocking collectives: 15.3 us -> none  [shards(): lax.all_to_all(asked_rows, 'dp', split_axis=0, concat_axis=0, tiled=True)]
    another operation x3 -> x0, local copies, waits for them, and re-layouts: 9.38 us -> none  [the longest x1 4.08 us: attend_block(): key_heads = key_rows.reshape(block_count, NLEN, head_count, HD)]
  transfers between devices with their start and end apart: 3 -> 0, of which waited for: 2 -> 0; matrix products, arithmetic and copies ran while one was open for 7% -> 0% of each run, Pallas kernels for 0% -> 0%
where the time goes in v1:
time: 148 us; the launch traced here: 147 us
  Pallas kernels  141 us (95%)
  local copies, waits for them, and re-layouts  4.15 us (3%)
  other arithmetic  2.3 us (2%)
    pallas_call x1, Pallas kernels, fused(): pl.pallas_call(kernel, out_shape=jax.ShapeDtypeStruct((TOK, D), BF), in_s...  141 us
    unnamed x3, local copies, waits for them, and re-layouts  3.81 us

profile of v1, /device:TPU:1, one launch (start us, length us, event | category | flops | bytes accessed | tf_op | source)
XLA Modules:
  0.0 147.1 jit_solution(1764761138171220936)
XLA Ops:
  0.0 0.7 broadcast_multiply_fusion
  0.7 0.1 copy.17
  0.8 0.1 mul.38
  0.9 0.8 copy.16
  1.6 0.1 broadcast_in_dim.30
  1.7 0.8 copy.15
  2.5 0.1 reshape.72
  2.6 0.2 convert_reduce_fusion
  2.7 0.6 bitcast_add_fusion.slot
  3.4 0.1 add_select_fusion
  3.4 0.8 select_reduce_fusion
  4.2 140.6 %shard_map.82 = bf16[128,4096]{1,0:T(8,128)(2,1)} custom-call(bf16[128,4096]{1,0:T(8,128)(2,1)} %tok.1, bf16[4096,256]{1,0:T(8,128)(2,1)} %wq.1, bf16[896,256]{1,0:T(8,128)(2,1)} %wk.1, bf16[896,256]{1,0:T(8,128)(2,1)} %wv.1, bf16[256,4096]{1,0:T(8,128)(2,1)} %wo.1, bf16[16,128,896]{2,1,0:T(8,128)(2,1)} %enc.1, s32[32,1,128]{2,1,0:T(1,128)} %bitcast.3, ...), custom_call_target="tpu_custom_call" | custom-call | tf_op jit(solution)/shard_map/pallas_call | solution.py:446
  144.8 2.3 %copy.19 = bf16[128,4096]{1,0:T(8,128)(2,1)} copy(bf16[128,4096]{1,0:T(8,128)(2,1)} %shard_map.82) | data formatting | bytes 2097152
  (3 shorter events, 0.0 us)

commit v2 on v1

v2 whole, which is shorter than its diff:
```python
import math

import jax
import jax.numpy as jnp
from jax import lax
from jax.experimental import pallas as pl
from jax.experimental.pallas import tpu as pltpu
from jax.sharding import PartitionSpec as P

MESH = pl.DeviceIdType.MESH
BF = jnp.bfloat16
F32 = jnp.float32
HD = 128
SPAN = 64
D = 4096
ENC = 896
TOK = 128
NX = 4
NZ = 8
NP = 32
ROWS = 16
E_COLS = ((0, 512), (512, 384))
QZ = 1024
QSPLIT = 288
QU = (D - QZ) // 16
OU = D // 16
SLOTS = ((1, 0), (1, 1), (2, 0), (2, 1), (3, 0), (3, 1), (0, 1))
OUT_CHUNK = 1024


def kernel(
    tok, wq, wk, wv, wo, enc, nbr_v, row_v, nbr_s, o_own, o_in,
    tokv, ttail, wqb, wkb, wvb, wob, band, ask_o, ask_r, rank_v, pick_v, pick_s, send_e, recv_a, recv_b, send_z, encz,
    qb, kb, vb, att, att0, acc, t_own, t_send, r_out, r_in,
    l_sem, sz, rz, sx, rx, es, e1r, e2r, e3r, st, rt,
):
    d = lax.axis_index("dp")
    z = lax.axis_index("mp")
    x = d // 8
    y = lax.rem(d // 2, 4)
    c = lax.rem(d, 2)
    other = (d + 1 - 2 * c, z)
    zdn = (d, lax.rem(z + 7, NZ))
    zup = (d, lax.rem(z + 1, NZ))
    odn = (other[0], zdn[1])
    oup = (other[0], zup[1])

    def plane(px, py):
        return (px * 8 + py * 2 + c, z)

    ring = {
        "x": (plane(lax.rem(x + 1, 4), y), plane(lax.rem(x + 3, 4), y)),
        "y": (plane(x, lax.rem(y + 1, 4)), plane(x, lax.rem(y + 3, 4))),
    }
    cs = pl.ds(pl.multiple_of(c * HD, HD), HD)

    def remote(src, dst, ssem, rsem, dev):
        return pltpu.make_async_remote_copy(
            src_ref=src, dst_ref=dst, send_sem=ssem, recv_sem=rsem, device_id=dev, device_id_type=MESH
        )

    half0 = pl.ds(0, HD)
    local = [
        pltpu.make_async_copy(enc.at[:, pl.ds(pl.multiple_of(z * ROWS, ROWS), ROWS), :], band, l_sem.at[0]),
        pltpu.make_async_copy(tok, tokv.at[pl.ds(0, TOK)], l_sem.at[1]),
        pltpu.make_async_copy(wq.at[:, cs], wqb.at[0, :, half0], l_sem.at[2]),
        pltpu.make_async_copy(wk.at[:, cs], wkb.at[0, :, half0], l_sem.at[3]),
        pltpu.make_async_copy(wv.at[:, cs], wvb.at[0, :, half0], l_sem.at[4]),
        pltpu.make_async_copy(wo.at[cs, :], wob.at[0, half0, :], l_sem.at[5]),
    ]
    for copy in local:
        copy.start()

    bar = pltpu.get_barrier_semaphore()

    def greet_plane(k, carry):
        pl.semaphore_signal(bar, inc=1, device_id=(lax.rem(d + k, NP), z), device_id_type=MESH)
        return carry

    def greet_z(k, carry):
        pl.semaphore_signal(bar, inc=1, device_id=(d, lax.rem(z + k, NZ)), device_id_type=MESH)
        return carry

    lax.fori_loop(1, NP, greet_plane, 0)
    lax.fori_loop(1, NZ, greet_z, 0)
    pl.semaphore_signal(bar, inc=1, device_id=odn, device_id_type=MESH)
    pl.semaphore_signal(bar, inc=1, device_id=oup, device_id_type=MESH)
    pl.semaphore_wait(bar, NP - 1 + NZ - 1 + 2)

    q_slice = (y * 4 + x, x * 4 + y)
    o_slice = (x * 4 + y, y * 4 + x)

    def q_at(sl, start, size):
        if sl is None:
            return wq.at[pl.ds(start, size), cs]
        return wqb.at[sl[0], pl.ds(start, size), pl.ds(sl[1] * HD, HD)]

    def o_at(sl, start, size):
        if sl is None:
            return wo.at[cs, pl.ds(start, size)]
        return wob.at[sl[0], pl.ds(sl[1] * HD, HD), pl.ds(start, size)]

    def kv_at(arg, buf, sl):
        if sl is None:
            return arg.at[:, cs]
        return buf.at[sl[0], :, pl.ds(sl[1] * HD, HD)]

    def drain(sem, units):
        if units <= D:
            ref = wqb.at[0, pl.ds(0, units), pl.ds(0, HD)]
        else:
            ref = wqb.at[pl.ds(0, 2), pl.ds(0, units // 2), pl.ds(0, HD)]
        pltpu.make_async_copy(ref, ref, sem).wait()

    SL, KV, Q0 = 0, 1, 2

    def z_start(k, part):
        for way in (0, 1):
            src_sl = None if k == 1 else (k - 1, way)
            dst_sl = (k, way) if k < 4 else (0, 1)
            pairs = []
            if part == SL and (k < 4 or way == 0):
                start = pl.multiple_of(QZ + q_slice[way] * QU, 16)
                pairs.append((q_at(src_sl, start, QU), q_at(dst_sl, start, QU)))
                start = pl.multiple_of(o_slice[way] * OU, 128)
                pairs.append((o_at(src_sl, start, OU), o_at(dst_sl, start, OU)))
            elif part == KV:
                if k < 4 or way == 0:
                    pairs.append((kv_at(wk, wkb, src_sl), kv_at(wk, wkb, dst_sl)))
                if k < 4 or way == 1:
                    pairs.append((kv_at(wv, wvb, src_sl), kv_at(wv, wvb, dst_sl)))
            elif part == Q0:
                start, size = (0, QZ) if k < 4 else ((0, QSPLIT) if way == 0 else (QSPLIT, QZ - QSPLIT))
                pairs.append((q_at(src_sl, start, size), q_at(dst_sl, start, size)))
            for src, dst in pairs:
                remote(src, dst, sz.at[k - 1, part], rz.at[k - 1, part], zup if way else zdn).start()

    def z_units(k, part):
        units = {SL: QU + OU, KV: 2 * ENC, Q0: QZ}[part]
        return 2 * units if k < 4 else units

    def z_wait(k, part):
        drain(rz.at[k - 1, part], z_units(k, part))

    def view(arr, sl, start, size):
        if arr == 0:
            return q_at(sl, pl.multiple_of(QZ + start, 16), size)
        return o_at(sl, pl.multiple_of(start, 128), size)

    def x_start(t, phase, arr):
        sl = SLOTS[t]
        u = (QU, OU)[arr]
        x_first = (arr == 0) == (t % 2 == 0)
        i1, i2 = (x, y) if x_first else (y, x)
        up, dn = ring["x" if x_first == (phase < 2) else "y"]
        if phase == 0:
            spans = [((i2 * 4 + i1) * u, u)] * 2
        elif phase == 1:
            spans = [
                ((i2 * 4 + lax.rem(i1 + 3, 4)) * u, u // 2),
                ((i2 * 4 + lax.rem(i1 + 1, 4)) * u + u // 2, u // 2),
            ]
        elif phase == 2:
            spans = [(i2 * 4 * u, 4 * u)] * 2
        else:
            spans = [
                (lax.rem(i2 + 3, 4) * 4 * u, 2 * u),
                (lax.rem(i2 + 1, 4) * 4 * u + 2 * u, 2 * u),
            ]
        for way, dev in enumerate((up, dn)):
            ref = view(arr, sl, *spans[way])
            remote(ref, ref, sx.at[t], rx.at[arr, t, phase], dev).start()

    def x_wait(t, phase, arr):
        drain(rx.at[arr, t, phase], 2 * (QU, OU)[arr] * (2, 1, 8, 4)[phase] // 2)

    def ph1(t):
        for arr in (0, 1):
            x_start(t, 0, arr)

    def step(t, phase, only=None):
        for arr in (0, 1) if only is None else (only,):
            x_wait(t, phase, arr)
            if phase < 3:
                x_start(t, phase + 1, arr)

    z_start(1, SL)
    last16 = pl.ds(TOK - 16, 16)
    tail_in = remote(tok.at[last16], ttail, st.at[0], rt.at[0], zup)
    tail_in.start()

    def each(n, f):
        def body(k, carry):
            f(k)
            return carry

        lax.fori_loop(1, n, body, 0)

    def whole(ref, sem):
        return pltpu.make_async_copy(ref, ref, sem)

    ask_o[...] = jnp.full((8, 128), -16, jnp.int32)
    ask_o[0:2, 0:16] = nbr_v[...] * 16 + row_v[...]

    def ask_copy(k):
        p = lax.rem(d + k, NP)
        remote(ask_o, ask_r.at[d], es.at[0], es.at[1], (p, z)).start()

    each(NP, ask_copy)
    ask_r[pl.ds(d, 1)] = ask_o[...][None]
    place = 2 * lax.broadcasted_iota(jnp.int32, (8, 128), 1) + lax.broadcasted_iota(jnp.int32, (8, 128), 0)
    mine = lax.shift_right_arithmetic(ask_o[...], 4)
    for f in range(32):
        same = jnp.logical_and(mine == nbr_s[f % 2, f // 2], place < f)
        rank_v[f] = jnp.where(same, 1, 0)
    rank = jnp.max(jnp.max(rank_v[...], axis=1, keepdims=True), axis=2, keepdims=True)
    pick_v[NP:, :, :] = jnp.broadcast_to(rank, (32, 1, 128))
    local[0].wait()
    whole(ask_r.at[pl.ds(0, NP - 1)], es.at[1]).wait()
    codes = ask_r[...]
    hit = lax.shift_right_arithmetic(codes, 4) == d
    key = place[None] * 16 + jnp.bitwise_and(codes, 15)
    low = jnp.where(hit, key, 1 << 20)
    low = jnp.min(jnp.min(low, axis=1, keepdims=True), axis=2, keepdims=True)
    high = jnp.where(hit, key, 0)
    high = jnp.max(jnp.max(high, axis=1, keepdims=True), axis=2, keepdims=True)
    lane = lax.broadcasted_iota(jnp.int32, (NP, 1, 128), 2)
    pick_v[:NP, :, :] = jnp.bitwise_and(jnp.where(lane == 0, low, high), 15)
    to_smem = pltpu.make_async_copy(pick_v, pick_s, l_sem.at[6])
    to_smem.start()
    to_smem.wait()

    recv_e = (recv_a, recv_b)

    def e1_start(part):
        cols = pl.ds(*E_COLS[part])

        def pick(s, carry):
            for j in range(2):
                send_e[s, j, :, cols] = band[pick_s[s, 0, j], :, cols]
            return carry

        lax.fori_loop(0, NP, pick, 0)

        def copy(k):
            p = lax.rem(d + k, NP)
            remote(
                send_e.at[p, :, :, cols], recv_e[part].at[pl.ds(2 * d, 2)], es.at[2], e1r.at[part], (p, z)
            ).start()

        each(NP, copy)
        recv_e[part][pl.ds(2 * d, 2)] = send_e[d, :, :, cols]

    my_rows = pl.ds(pl.multiple_of(z * ROWS, ROWS), ROWS)

    def e2_start(part):
        cols = pl.ds(*E_COLS[part])
        whole(recv_e[part].at[pl.ds(0, 2 * NP - 2)], e1r.at[part]).wait()

        def pick(mz, carry):
            spans = (lax.rem(2 * mz + 15, 16), 2 * mz)
            for i in range(4):
                span, n = spans[i // 2], i % 2
                place = 2 * nbr_s[n, span] + pick_s[NP + 2 * span + n, 0, 0]
                send_z[mz, i, :, cols] = recv_e[part][place]
            return carry

        lax.fori_loop(0, NZ, pick, 0)

        def copy(k):
            p = lax.rem(z + k, NZ)
            remote(
                send_z.at[p, :, :, cols], encz.at[pl.ds(0, 4), my_rows, cols], es.at[4], e2r.at[part], (d, p)
            ).start()

        each(NZ, copy)
        encz[pl.ds(0, 4), my_rows, cols] = send_z[z, :, :, cols]

    def e3_copy(part):
        cols = pl.ds(*E_COLS[part])
        return remote(encz.at[pl.ds(0, 4), :, cols], encz.at[pl.ds(4, 4), :, cols], es.at[6], e3r.at[part], other)

    def e3_start(part):
        cols = pl.ds(*E_COLS[part])
        whole(send_z.at[pl.ds(0, NZ - 1), :, :, cols], e2r.at[part]).wait()
        e3_copy(part).start()

    for part in range(len(E_COLS)):
        e1_start(part)
    z_wait(1, SL)
    z_start(2, SL)
    ph1(0)
    ph1(1)
    z_start(1, KV)
    z_start(1, Q0)

    local[1].wait()
    tail_in.wait_recv()
    is15 = lax.broadcasted_iota(jnp.int32, (16, D), 0) == 15
    tokv[TOK - 16 : TOK, :] = jnp.where(is15, ttail[...], tokv[TOK - 16 : TOK, :])
    tok_x = remote(tokv.at[pl.ds(0, TOK)], tokv.at[pl.ds(TOK, TOK)], st.at[1], rt.at[1], other)
    tok_x.start()
    z_wait(2, SL)
    z_start(3, SL)
    ph1(2)
    ph1(3)
    z_wait(3, SL)
    z_start(4, SL)
    ph1(4)
    ph1(5)
    z_wait(4, SL)
    ph1(6)

    def project(pair, half):
        lanes = pl.ds(0, 256) if half is None else pl.ds(half * HD, HD)
        width = 256 if half is None else HD

        def body(k, total):
            start = pl.multiple_of(k * 2048, 2048)
            return total + jnp.dot(
                tokv[:, pl.ds(start, 2048)], wqb[pair, pl.ds(start, 2048), lanes], preferred_element_type=F32
            )

        total = lax.fori_loop(0, D // 2048, body, jnp.zeros((2 * TOK, width), F32))
        qb[pair, :, lanes] = total.astype(BF)

    def keys_values(pair, half):
        lanes = pl.ds(0, 256) if half is None else pl.ds(half * HD, HD)

        def body(u, carry):
            rows = encz[pl.ds(4 * u, 4)].reshape(512, ENC)
            keys = jnp.dot(rows, wkb[pair, :, lanes], preferred_element_type=F32)
            kb[pl.ds(2 * u, 2), :, lanes] = keys.astype(BF).reshape(2, 256, -1)
            values = jnp.dot(rows, wvb[pair, :, lanes], preferred_element_type=F32)
            vb[pl.ds(2 * u, 2), :, lanes] = values.astype(BF).reshape(2, 256, -1)
            return carry

        lax.fori_loop(0, 2, body, 0)

    row_id = lax.broadcasted_iota(jnp.int32, (TOK, 256), 0)
    in_b = jnp.logical_and(row_id >= SPAN - 1, row_id < TOK - 1)
    blank = jnp.logical_and(lax.broadcasted_iota(jnp.int32, (TOK, HD), 0) < SPAN - 1, z == 0)

    def attend(pair, half, dst):
        halves = (0, 1) if half is None else (half,)
        for s in range(2):
            for h in halves:
                lanes = pl.ds(h * HD, HD)
                q = qb[pair, s * TOK : (s + 1) * TOK, lanes]
                ka, kb_ = kb[2 * s, :, lanes], kb[2 * s + 1, :, lanes]
                dims = (((1,), (1,)), ((), ()))
                sa_ = lax.dot_general(q, ka, dims, preferred_element_type=F32)
                sb_ = lax.dot_general(q, kb_, dims, preferred_element_type=F32)
                scores = jnp.where(in_b, sb_, sa_) * F32(1.0 / math.sqrt(HD))
                peak = jnp.max(scores, axis=1, keepdims=True)
                e = jnp.exp(scores - peak)
                total = jnp.sum(e, axis=1, keepdims=True)
                wa = jnp.where(in_b, 0.0, e).astype(BF)
                wb = jnp.where(in_b, e, 0.0).astype(BF)
                o = jnp.dot(wa, vb[2 * s, :, lanes], preferred_element_type=F32)
                o = o + jnp.dot(wb, vb[2 * s + 1, :, lanes], preferred_element_type=F32)
                o = jnp.where(blank, 0.0, o / total)
                dst[s * TOK : (s + 1) * TOK, lanes] = o.astype(BF)

    def add_out(pair, is_first):
        def body(k, carry):
            cols = pl.ds(pl.multiple_of(k * OUT_CHUNK, OUT_CHUNK), OUT_CHUNK)
            term = jnp.dot(att[...], wob[pair, :, cols], preferred_element_type=F32)
            acc[:, cols] = term if is_first else acc[:, cols] + term
            return carry

        lax.fori_loop(0, D // OUT_CHUNK, body, 0)

    step(0, 0)
    step(1, 0)
    step(2, 0)
    step(3, 0)
    z_wait(1, KV)
    z_start(2, KV)
    step(4, 0)
    step(5, 0)
    step(6, 0)
    step(0, 1)
    z_wait(1, Q0)
    z_start(2, Q0)
    step(1, 1)
    tok_x.wait_recv()
    local[2].wait()
    project(0, 0)
    step(2, 1)
    e2_start(0)
    e2_start(1)
    z_wait(2, KV)
    z_start(3, KV)
    step(3, 1)
    step(0, 2)
    z_wait(2, Q0)
    z_start(3, Q0)
    step(1, 2)
    step(4, 1)
    step(2, 2)
    step(5, 1)
    step(0, 3)
    step(1, 3)
    project(1, None)
    step(3, 2)
    step(6, 1)
    e3_start(0)
    e3_start(1)
    for part in range(len(E_COLS)):
        e3_copy(part).wait_recv()
    local[3].wait()
    local[4].wait()
    local[5].wait()
    whole(ask_r.at[pl.ds(0, NP - 1)], es.at[0]).wait()
    whole(send_e.at[pl.ds(0, NP - 1)], es.at[2]).wait()
    tail_in.wait_send()
    tok_x.wait_send()
    step(2, 3)
    keys_values(0, 0)
    attend(0, 0, att0)
    z_wait(3, KV)
    z_start(4, KV)
    keys_values(1, None)
    step(4, 2)
    attend(1, None, att)
    add_out(1, True)
    z_wait(3, Q0)
    z_start(4, Q0)
    step(3, 3)
    project(2, None)
    keys_values(2, None)
    step(5, 2)
    attend(2, None, att)
    add_out(2, False)
    step(4, 3)
    step(6, 2)
    step(5, 3)
    project(3, None)
    keys_values(3, None)
    attend(3, None, att)
    add_out(3, False)
    whole(send_z.at[pl.ds(0, NZ - 1)], es.at[4]).wait()
    whole(encz.at[pl.ds(0, 4)], es.at[6]).wait()
    for k in range(1, 4):
        for part in (SL, KV, Q0):
            drain(sz.at[k - 1, part], z_units(k, part))
    for t in range(6):
        drain(sx.at[t], 15 * (QU + OU))
    z_wait(4, KV)
    keys_values(0, 1)
    z_wait(4, Q0)
    step(6, 3)
    project(0, 1)
    attend(0, 1, att0)

    def last(k, carry):
        cols = pl.ds(pl.multiple_of(k * OUT_CHUNK, OUT_CHUNK), OUT_CHUNK)
        term = acc[:, cols] + jnp.dot(att0[...], wob[0, :, cols], preferred_element_type=F32)
        term = term.astype(BF)
        edge15 = lax.broadcasted_iota(jnp.int32, (16, OUT_CHUNK), 0) == 15
        for s, buf in enumerate((t_own, t_send)):
            edge = term[(s + 1) * TOK - 16 : (s + 1) * TOK]
            buf[0 : TOK - 16, cols] = term[s * TOK : (s + 1) * TOK - 16]
            buf[TOK - 16 : TOK, cols] = jnp.where(edge15, jnp.zeros_like(edge), edge)
            r_out[s, :, cols] = edge
        remote(t_send.at[:, cols], o_in.at[:, cols], st.at[3], rt.at[3], other).start()
        remote(r_out.at[0, :, cols], r_in.at[0, :, cols], st.at[4], rt.at[4], zdn).start()
        remote(r_out.at[1, :, cols], r_in.at[1, :, cols], st.at[5], rt.at[5], odn).start()
        top = pl.ds(0, TOK - 16)
        pltpu.make_async_copy(t_own.at[top, cols], o_own.at[top, cols], l_sem.at[7]).start()
        return carry

    lax.fori_loop(0, D // OUT_CHUNK, last, 0)
    for part in (SL, KV, Q0):
        drain(sz.at[3, part], z_units(4, part))
    drain(sx.at[6], 15 * (QU + OU))
    whole(r_in.at[0], rt.at[4]).wait()
    whole(r_in.at[1], rt.at[5]).wait()
    edge = (r_in[0].astype(F32) + r_in[1].astype(F32)).astype(BF)
    t_own[TOK - 16 : TOK, :] = jnp.where(is15, edge, t_own[TOK - 16 : TOK, :])
    bottom = pltpu.make_async_copy(t_own.at[last16], o_own.at[last16], l_sem.at[6])
    bottom.start()
    whole(t_own.at[pl.ds(0, TOK - 16)], l_sem.at[7]).wait()
    whole(r_out.at[0], st.at[4]).wait()
    whole(r_out.at[1], st.at[5]).wait()
    whole(t_send, st.at[3]).wait()
    whole(o_in, rt.at[3]).wait()
    bottom.wait()


def fused(tokens, w_query, w_key, w_value, w_out, encoded, nbr_shard, nbr_row):
    any_ = pl.BlockSpec(memory_space=pl.ANY)
    vmem = pl.BlockSpec(memory_space=pltpu.VMEM)
    smem = pl.BlockSpec(memory_space=pltpu.SMEM)
    dma = pltpu.SemaphoreType.DMA
    V = pltpu.VMEM
    return pl.pallas_call(
        kernel,
        out_shape=(jax.ShapeDtypeStruct((TOK, D), BF), jax.ShapeDtypeStruct((TOK, D), BF)),
        in_specs=[any_] * 6 + [vmem, vmem, smem],
        out_specs=(any_, any_),
        scratch_shapes=[
            V((2 * TOK, D), BF),
            V((16, D), BF),
            V((4, D, 256), BF),
            V((4, ENC, 256), BF),
            V((4, ENC, 256), BF),
            V((4, 256, D), BF),
            V((16, ROWS, ENC), BF),
            V((8, 128), jnp.int32),
            V((NP, 8, 128), jnp.int32),
            V((32, 8, 128), jnp.int32),
            V((2 * NP, 1, 128), jnp.int32),
            pltpu.SMEM((2 * NP, 1, 128), jnp.int32),
            V((NP, 2, ROWS, ENC), BF),
            V((2 * NP, ROWS, E_COLS[0][1]), BF),
            V((2 * NP, ROWS, E_COLS[1][1]), BF),
            V((NZ, 4, ROWS, ENC), BF),
            V((8, 128, ENC), BF),
            V((4, 2 * TOK, 256), BF),
            V((4, 256, 256), BF),
            V((4, 256, 256), BF),
            V((2 * TOK, 256), BF),
            V((2 * TOK, 256), BF),
            V((2 * TOK, D), F32),
            V((TOK, D), BF),
            V((TOK, D), BF),
            V((2, 16, D), BF),
            V((2, 16, D), BF),
            dma((8,)),
            dma((4, 3)),
            dma((4, 3)),
            dma((7,)),
            dma((2, 7, 4)),
            dma((7,)),
            dma((len(E_COLS),)),
            dma((len(E_COLS),)),
            dma((len(E_COLS),)),
            dma((6,)),
            dma((6,)),
        ],
        compiler_params=pltpu.CompilerParams(
            collective_id=0, has_side_effects=True, vmem_limit_bytes=56 * 1024 * 1024
        ),
    )(tokens, w_query, w_key, w_value, w_out, encoded, nbr_shard, nbr_row, nbr_shard)


def shards(tokens, w_query, w_key, w_value, w_out, encoded, nbr_shard, nbr_row):
    own, received = fused(
        tokens, w_query, w_key, w_value, w_out, encoded, nbr_shard.T, nbr_row.T
    )
    return (own.astype(F32) + received.astype(F32)).astype(BF)


def solution(mesh):
    return jax.shard_map(
        shards,
        mesh=mesh,
        in_specs=(
            P(("dp", "mp"), None),
            P(None, "mp"),
            P(None, "mp"),
            P(None, "mp"),
            P("mp", None),
            P("dp", None, None),
            P("dp", None),
            P("dp", None),
        ),
        out_specs=P(("dp", "mp"), None),
        check_vma=False,
    )
```

time: 148 us -> 127 us (0.86)
  Pallas kernels: 141 us -> 123 us
  local copies, waits for them, and re-layouts: 4.15 us -> 0 us
    pallas_call x1, Pallas kernels: 141 us -> 123 us  [fused(): pl.pallas_call(kernel, out_shape=(jax.ShapeDtypeStruct((TOK, D), BF), jax...]
    unnamed x3 -> x0, local copies, waits for them, and re-layouts: 3.81 us -> none
    convert_element_type x0 -> x1, other arithmetic: none -> 2.76 us  [shards(): return (own.astype(F32) + received.astype(F32)).astype(BF)]
where the time goes in v2:
time: 127 us; the launch traced here: 126 us
  Pallas kernels  123 us (97%)
  other arithmetic  2.76 us (2%)
    pallas_call x1, Pallas kernels, fused(): pl.pallas_call(kernel, out_shape=(jax.ShapeDtypeStruct((TOK, D), BF), jax...  123 us
    convert_element_type x1, other arithmetic, shards(): return (own.astype(F32) + received.astype(F32)).astype(BF)  2.76 us

profile of v2, /device:TPU:1, one launch (start us, length us, event | category | flops | bytes accessed | tf_op | source)
XLA Modules:
  0.0 126.1 jit_solution(6664604621274086056)
XLA Ops:
  0.0 123.3 %shard_map.82 = (bf16[128,4096]{1,0:T(8,128)(2,1)}, bf16[128,4096]{1,0:T(8,128)(2,1)}) custom-call(bf16[128,4096]{1,0:T(8,128)(2,1)} %tok.1, bf16[4096,256]{1,0:T(8,128)(2,1)} %wq.1, bf16[896,256]{1,0:T(8,128)(2,1)} %wk.1, bf16[896,256]{1,0:T(8,128)(2,1)} %wv.1, bf16[256,4096]{1,0:T(8,128)(2,1)} %wo.1, bf16[16,128,896]{2,1,0:T(8,128)(2,1)} %enc.1, ...), custom_call_target="tpu_custom_call" | custom-call | tf_op jit(solution)/shard_map/pallas_call | solution.py:498
  123.3 2.8 %add_convert_fusion = bf16[128,4096]{1,0:T(8,128)(2,1)} fusion(bf16[128,4096]{1,0:T(8,128)(2,1)} %get-tuple-element.8, bf16[128,4096]{1,0:T(8,128)(2,1)} %get-tuple-element.7), kind=kLoop, calls=%fused_computation | loop fusion | flops 2097152 | bytes 3145728 | tf_op jit(solution)/shard_map/convert_element_type | solution.py:553

commit v3 on v2

--- a/solution.py
+++ b/solution.py
@@ -30,8 +30,8 @@
 
 def kernel(
     tok, wq, wk, wv, wo, enc, nbr_v, row_v, nbr_s, o_own, o_in,
-    tokv, ttail, wqb, wkb, wvb, wob, band, ask_o, ask_r, rank_v, pick_v, pick_s, send_e, recv_a, recv_b, send_z, encz,
-    qb, kb, vb, att, att0, acc, t_own, t_send, r_out, r_in,
+    tokv, e_out, e_in, wqb, wkb, wvb, wob, band, ask_o, ask_r, rank_v, pick_v, pick_s, send_e, recv_a, recv_b, send_z, encz,
+    qb, kb, vb, att, att0, acc, t_own, t_send, r_out,
     l_sem, sz, rz, sx, rx, es, e1r, e2r, e3r, st, rt,
 ):
     d = lax.axis_index("dp")
@@ -186,8 +186,21 @@
 
     z_start(1, SL)
     last16 = pl.ds(TOK - 16, 16)
-    tail_in = remote(tok.at[last16], ttail, st.at[0], rt.at[0], zup)
-    tail_in.start()
+    is15 = lax.broadcasted_iota(jnp.int32, (16, 256), 0) == 15
+
+    def fold(rows, i):
+        row = rows.astype(F32)[15:16, :]
+        packed = jnp.zeros((16, 256), F32)
+        for j in range(16):
+            piece = jnp.broadcast_to(row[:, 256 * j : 256 * (j + 1)], (16, 256))
+            packed = jnp.where(lax.broadcasted_iota(jnp.int32, (16, 256), 0) == j, piece, packed)
+        e_out[i] = packed.astype(BF)
+
+    def unfold(packed, buf):
+        for j in range(16):
+            cols = pl.ds(256 * j, 256)
+            piece = jnp.broadcast_to(packed[j : j + 1, :], (16, 256))
+            buf[TOK - 16 : TOK, cols] = jnp.where(is15, piece, buf[TOK - 16 : TOK, cols].astype(F32)).astype(BF)
 
     def each(n, f):
         def body(k, carry):
@@ -207,6 +220,12 @@
         remote(ask_o, ask_r.at[d], es.at[0], es.at[1], (p, z)).start()
 
     each(NP, ask_copy)
+    z_start(1, KV)
+    z_start(1, Q0)
+    local[1].wait()
+    fold(tokv[TOK - 16 : TOK, :], 0)
+    tail_in = remote(e_out.at[0], e_in.at[0], st.at[0], rt.at[0], zup)
+    tail_in.start()
     ask_r[pl.ds(d, 1)] = ask_o[...][None]
     place = 2 * lax.broadcasted_iota(jnp.int32, (8, 128), 1) + lax.broadcasted_iota(jnp.int32, (8, 128), 0)
     mine = lax.shift_right_arithmetic(ask_o[...], 4)
@@ -215,6 +234,10 @@
         rank_v[f] = jnp.where(same, 1, 0)
     rank = jnp.max(jnp.max(rank_v[...], axis=1, keepdims=True), axis=2, keepdims=True)
     pick_v[NP:, :, :] = jnp.broadcast_to(rank, (32, 1, 128))
+    z_wait(1, SL)
+    z_start(2, SL)
+    ph1(0)
+    ph1(1)
     local[0].wait()
     whole(ask_r.at[pl.ds(0, NP - 1)], es.at[1]).wait()
     codes = ask_r[...]
@@ -287,17 +310,9 @@
 
     for part in range(len(E_COLS)):
         e1_start(part)
-    z_wait(1, SL)
-    z_start(2, SL)
-    ph1(0)
-    ph1(1)
-    z_start(1, KV)
-    z_start(1, Q0)
-
-    local[1].wait()
+
     tail_in.wait_recv()
-    is15 = lax.broadcasted_iota(jnp.int32, (16, D), 0) == 15
-    tokv[TOK - 16 : TOK, :] = jnp.where(is15, ttail[...], tokv[TOK - 16 : TOK, :])
+    unfold(e_in[0].astype(F32), tokv)
     tok_x = remote(tokv.at[pl.ds(0, TOK)], tokv.at[pl.ds(TOK, TOK)], st.at[1], rt.at[1], other)
     tok_x.start()
     z_wait(2, SL)
@@ -393,9 +408,9 @@
     z_wait(2, KV)
     z_start(3, KV)
     step(3, 1)
-    step(0, 2)
     z_wait(2, Q0)
     z_start(3, Q0)
+    step(0, 2)
     step(1, 2)
     step(4, 1)
     step(2, 2)
@@ -417,10 +432,10 @@
     tail_in.wait_send()
     tok_x.wait_send()
     step(2, 3)
+    z_wait(3, KV)
+    z_start(4, KV)
     keys_values(0, 0)
     attend(0, 0, att0)
-    z_wait(3, KV)
-    z_start(4, KV)
     keys_values(1, None)
     step(4, 2)
     attend(1, None, att)
@@ -430,16 +445,23 @@
     step(3, 3)
     project(2, None)
     keys_values(2, None)
-    step(5, 2)
+    step(5, 2, 0)
+    step(6, 2, 0)
+    step(5, 2, 1)
     attend(2, None, att)
     add_out(2, False)
     step(4, 3)
-    step(6, 2)
-    step(5, 3)
+    step(6, 2, 1)
+    step(5, 3, 0)
     project(3, None)
     keys_values(3, None)
     attend(3, None, att)
-    add_out(3, False)
+    step(6, 3, 0)
+    z_wait(4, KV)
+    z_wait(4, Q0)
+    keys_values(0, 1)
+    project(0, 1)
+    attend(0, 1, att0)
     whole(send_z.at[pl.ds(0, NZ - 1)], es.at[4]).wait()
     whole(encz.at[pl.ds(0, 4)], es.at[6]).wait()
     for k in range(1, 4):
@@ -447,16 +469,13 @@
             drain(sz.at[k - 1, part], z_units(k, part))
     for t in range(6):
         drain(sx.at[t], 15 * (QU + OU))
-    z_wait(4, KV)
-    keys_values(0, 1)
-    z_wait(4, Q0)
-    step(6, 3)
-    project(0, 1)
-    attend(0, 1, att0)
+    step(5, 3, 1)
+    step(6, 3, 1)
 
     def last(k, carry):
         cols = pl.ds(pl.multiple_of(k * OUT_CHUNK, OUT_CHUNK), OUT_CHUNK)
-        term = acc[:, cols] + jnp.dot(att0[...], wob[0, :, cols], preferred_element_type=F32)
+        term = acc[:, cols] + jnp.dot(att[...], wob[3, :, cols], preferred_element_type=F32)
+        term = term + jnp.dot(att0[...], wob[0, :, cols], preferred_element_type=F32)
         term = term.astype(BF)
         edge15 = lax.broadcasted_iota(jnp.int32, (16, OUT_CHUNK), 0) == 15
         for s, buf in enumerate((t_own, t_send)):
@@ -465,25 +484,27 @@
             buf[TOK - 16 : TOK, cols] = jnp.where(edge15, jnp.zeros_like(edge), edge)
             r_out[s, :, cols] = edge
         remote(t_send.at[:, cols], o_in.at[:, cols], st.at[3], rt.at[3], other).start()
-        remote(r_out.at[0, :, cols], r_in.at[0, :, cols], st.at[4], rt.at[4], zdn).start()
-        remote(r_out.at[1, :, cols], r_in.at[1, :, cols], st.at[5], rt.at[5], odn).start()
         top = pl.ds(0, TOK - 16)
         pltpu.make_async_copy(t_own.at[top, cols], o_own.at[top, cols], l_sem.at[7]).start()
         return carry
 
     lax.fori_loop(0, D // OUT_CHUNK, last, 0)
+    edges = []
+    for i, dev in ((1, zdn), (2, odn)):
+        fold(r_out[i - 1], i)
+        edges.append(remote(e_out.at[i], e_in.at[i], st.at[i + 3], rt.at[i + 3], dev))
+        edges[-1].start()
     for part in (SL, KV, Q0):
         drain(sz.at[3, part], z_units(4, part))
     drain(sx.at[6], 15 * (QU + OU))
-    whole(r_in.at[0], rt.at[4]).wait()
-    whole(r_in.at[1], rt.at[5]).wait()
-    edge = (r_in[0].astype(F32) + r_in[1].astype(F32)).astype(BF)
-    t_own[TOK - 16 : TOK, :] = jnp.where(is15, edge, t_own[TOK - 16 : TOK, :])
+    for edge in edges:
+        edge.wait_recv()
+    unfold(e_in[1].astype(F32) + e_in[2].astype(F32), t_own)
     bottom = pltpu.make_async_copy(t_own.at[last16], o_own.at[last16], l_sem.at[6])
     bottom.start()
     whole(t_own.at[pl.ds(0, TOK - 16)], l_sem.at[7]).wait()
-    whole(r_out.at[0], st.at[4]).wait()
-    whole(r_out.at[1], st.at[5]).wait()
+    for edge in edges:
+        edge.wait_send()
     whole(t_send, st.at[3]).wait()
     whole(o_in, rt.at[3]).wait()
     bottom.wait()
@@ -502,7 +523,8 @@
         out_specs=(any_, any_),
         scratch_shapes=[
             V((2 * TOK, D), BF),
-            V((16, D), BF),
+            V((3, 16, 256), BF),
+            V((3, 16, 256), BF),
             V((4, D, 256), BF),
             V((4, ENC, 256), BF),
             V((4, ENC, 256), BF),
@@ -527,7 +549,6 @@
             V((TOK, D), BF),
             V((TOK, D), BF),
             V((2, 16, D), BF),
-            V((2, 16, D), BF),
             dma((8,)),
             dma((4, 3)),
             dma((4, 3)),

time: 127 us -> 122 us (0.961)
  Pallas kernels: 123 us -> 119 us
    pallas_call x1, Pallas kernels: 123 us -> 119 us  [fused(): pl.pallas_call(kernel, out_shape=(jax.ShapeDtypeStruct((TOK, D), BF), jax...]
where the time goes in v3:
time: 122 us
  Pallas kernels  119 us (98%)
  other arithmetic  2.76 us (2%)
    pallas_call x1, Pallas kernels, fused(): pl.pallas_call(kernel, out_shape=(jax.ShapeDtypeStruct((TOK, D), BF), jax...  119 us
    convert_element_type x1, other arithmetic, shards(): return (own.astype(F32) + received.astype(F32)).astype(BF)  2.76 us

profile of v3, /device:TPU:1, one launch (start us, length us, event | category | flops | bytes accessed | tf_op | source)
XLA Modules:
  0.0 121.6 jit_solution(11083506070160710751)
XLA Ops:
  0.0 118.8 %shard_map.82 = (bf16[128,4096]{1,0:T(8,128)(2,1)}, bf16[128,4096]{1,0:T(8,128)(2,1)}) custom-call(bf16[128,4096]{1,0:T(8,128)(2,1)} %tok.1, bf16[4096,256]{1,0:T(8,128)(2,1)} %wq.1, bf16[896,256]{1,0:T(8,128)(2,1)} %wk.1, bf16[896,256]{1,0:T(8,128)(2,1)} %wv.1, bf16[256,4096]{1,0:T(8,128)(2,1)} %wo.1, bf16[16,128,896]{2,1,0:T(8,128)(2,1)} %enc.1, ...), custom_call_target="tpu_custom_call" | custom-call | tf_op jit(solution)/shard_map/pallas_call | solution.py:519
  118.8 2.8 %add_convert_fusion = bf16[128,4096]{1,0:T(8,128)(2,1)} fusion(bf16[128,4096]{1,0:T(8,128)(2,1)} %get-tuple-element.8, bf16[128,4096]{1,0:T(8,128)(2,1)} %get-tuple-element.7), kind=kLoop, calls=%fused_computation | loop fusion | flops 2097152 | bytes 3145728 | tf_op jit(solution)/shard_map/convert_element_type | solution.py:574

commit v4 on v3

--- a/solution.py
+++ b/solution.py
@@ -19,7 +19,7 @@
 NZ = 8
 NP = 32
 ROWS = 16
-E_COLS = ((0, 512), (512, 384))
+E_COLS = ((0, 384), (384, 256), (640, 256))
 QZ = 1024
 QSPLIT = 288
 QU = (D - QZ) // 16
@@ -30,7 +30,7 @@
 
 def kernel(
     tok, wq, wk, wv, wo, enc, nbr_v, row_v, nbr_s, o_own, o_in,
-    tokv, e_out, e_in, wqb, wkb, wvb, wob, band, ask_o, ask_r, rank_v, pick_v, pick_s, send_e, recv_a, recv_b, send_z, encz,
+    tokv, e_out, e_in, wqb, wkb, wvb, wob, band, ask_o, ask_r, rank_v, pick_v, pick_s, send_e, recv_a, recv_b, recv_c, send_z, encz,
     qb, kb, vb, att, att0, acc, t_own, t_send, r_out,
     l_sem, sz, rz, sx, rx, es, e1r, e2r, e3r, st, rt,
 ):
@@ -253,7 +253,7 @@
     to_smem.start()
     to_smem.wait()
 
-    recv_e = (recv_a, recv_b)
+    recv_e = (recv_a, recv_b, recv_c)
 
     def e1_start(part):
         cols = pl.ds(*E_COLS[part])
@@ -402,9 +402,10 @@
     tok_x.wait_recv()
     local[2].wait()
     project(0, 0)
+    e2_start(0)
     step(2, 1)
-    e2_start(0)
     e2_start(1)
+    e2_start(2)
     z_wait(2, KV)
     z_start(3, KV)
     step(3, 1)
@@ -422,6 +423,7 @@
     step(6, 1)
     e3_start(0)
     e3_start(1)
+    e3_start(2)
     for part in range(len(E_COLS)):
         e3_copy(part).wait_recv()
     local[3].wait()
@@ -456,19 +458,12 @@
     project(3, None)
     keys_values(3, None)
     attend(3, None, att)
+    z_wait(4, KV)
+    keys_values(0, 1)
     step(6, 3, 0)
-    z_wait(4, KV)
     z_wait(4, Q0)
-    keys_values(0, 1)
     project(0, 1)
     attend(0, 1, att0)
-    whole(send_z.at[pl.ds(0, NZ - 1)], es.at[4]).wait()
-    whole(encz.at[pl.ds(0, 4)], es.at[6]).wait()
-    for k in range(1, 4):
-        for part in (SL, KV, Q0):
-            drain(sz.at[k - 1, part], z_units(k, part))
-    for t in range(6):
-        drain(sx.at[t], 15 * (QU + OU))
     step(5, 3, 1)
     step(6, 3, 1)
 
@@ -494,6 +489,13 @@
         fold(r_out[i - 1], i)
         edges.append(remote(e_out.at[i], e_in.at[i], st.at[i + 3], rt.at[i + 3], dev))
         edges[-1].start()
+    whole(send_z.at[pl.ds(0, NZ - 1)], es.at[4]).wait()
+    whole(encz.at[pl.ds(0, 4)], es.at[6]).wait()
+    for k in range(1, 4):
+        for part in (SL, KV, Q0):
+            drain(sz.at[k - 1, part], z_units(k, part))
+    for t in range(6):
+        drain(sx.at[t], 15 * (QU + OU))
     for part in (SL, KV, Q0):
         drain(sz.at[3, part], z_units(4, part))
     drain(sx.at[6], 15 * (QU + OU))
@@ -538,6 +540,7 @@
             V((NP, 2, ROWS, ENC), BF),
             V((2 * NP, ROWS, E_COLS[0][1]), BF),
             V((2 * NP, ROWS, E_COLS[1][1]), BF),
+            V((2 * NP, ROWS, E_COLS[2][1]), BF),
             V((NZ, 4, ROWS, ENC), BF),
             V((8, 128, ENC), BF),
             V((4, 2 * TOK, 256), BF),

time: 122 us -> 120 us (0.984)
  Pallas kernels: 119 us -> 117 us
    pallas_call x1, Pallas kernels: 119 us -> 117 us  [fused(): pl.pallas_call(kernel, out_shape=(jax.ShapeDtypeStruct((TOK, D), BF), jax...]
where the time goes in v4:
time: 120 us
  Pallas kernels  117 us (98%)
  other arithmetic  2.76 us (2%)
    pallas_call x1, Pallas kernels, fused(): pl.pallas_call(kernel, out_shape=(jax.ShapeDtypeStruct((TOK, D), BF), jax...  117 us
    convert_element_type x1, other arithmetic, shards(): return (own.astype(F32) + received.astype(F32)).astype(BF)  2.76 us

profile of v4, /device:TPU:1, one launch (start us, length us, event | category | flops | bytes accessed | tf_op | source)
XLA Modules:
  0.0 120.1 jit_solution(1371720919218722726)
XLA Ops:
  0.0 117.4 %shard_map.82 = (bf16[128,4096]{1,0:T(8,128)(2,1)}, bf16[128,4096]{1,0:T(8,128)(2,1)}) custom-call(bf16[128,4096]{1,0:T(8,128)(2,1)} %tok.1, bf16[4096,256]{1,0:T(8,128)(2,1)} %wq.1, bf16[896,256]{1,0:T(8,128)(2,1)} %wk.1, bf16[896,256]{1,0:T(8,128)(2,1)} %wv.1, bf16[256,4096]{1,0:T(8,128)(2,1)} %wo.1, bf16[16,128,896]{2,1,0:T(8,128)(2,1)} %enc.1, ...), custom_call_target="tpu_custom_call" | custom-call | tf_op jit(solution)/shard_map/pallas_call | solution.py:521
  117.4 2.8 %add_convert_fusion = bf16[128,4096]{1,0:T(8,128)(2,1)} fusion(bf16[128,4096]{1,0:T(8,128)(2,1)} %get-tuple-element.8, bf16[128,4096]{1,0:T(8,128)(2,1)} %get-tuple-element.7), kind=kLoop, calls=%fused_computation | loop fusion | flops 2097152 | bytes 3145728 | tf_op jit(solution)/shard_map/convert_element_type | solution.py:577

commit v5 on v4

--- a/solution.py
+++ b/solution.py
@@ -25,7 +25,7 @@
 QU = (D - QZ) // 16
 OU = D // 16
 SLOTS = ((1, 0), (1, 1), (2, 0), (2, 1), (3, 0), (3, 1), (0, 1))
-OUT_CHUNK = 1024
+OUT_CHUNK = 2048
 
 
 def kernel(
@@ -331,12 +331,12 @@
         width = 256 if half is None else HD
 
         def body(k, total):
-            start = pl.multiple_of(k * 2048, 2048)
+            start = pl.multiple_of(k * D, D)
             return total + jnp.dot(
-                tokv[:, pl.ds(start, 2048)], wqb[pair, pl.ds(start, 2048), lanes], preferred_element_type=F32
+                tokv[:, pl.ds(start, D)], wqb[pair, pl.ds(start, D), lanes], preferred_element_type=F32
             )
 
-        total = lax.fori_loop(0, D // 2048, body, jnp.zeros((2 * TOK, width), F32))
+        total = lax.fori_loop(0, 1, body, jnp.zeros((2 * TOK, width), F32))
         qb[pair, :, lanes] = total.astype(BF)
 
     def keys_values(pair, half):

time: 120 us -> 119 us (level)
  no operation moved by 1% of the time
where the time goes in v5:
time: 119 us
  Pallas kernels  116 us (97%)
  other arithmetic  2.76 us (2%)
    pallas_call x1, Pallas kernels, fused(): pl.pallas_call(kernel, out_shape=(jax.ShapeDtypeStruct((TOK, D), BF), jax...  116 us
    convert_element_type x1, other arithmetic, shards(): return (own.astype(F32) + received.astype(F32)).astype(BF)  2.76 us

profile of v5, /device:TPU:1, one launch (start us, length us, event | category | flops | bytes accessed | tf_op | source)
XLA Modules:
  0.0 119.0 jit_solution(2454743036873251087)
XLA Ops:
  0.0 116.2 %shard_map.82 = (bf16[128,4096]{1,0:T(8,128)(2,1)}, bf16[128,4096]{1,0:T(8,128)(2,1)}) custom-call(bf16[128,4096]{1,0:T(8,128)(2,1)} %tok.1, bf16[4096,256]{1,0:T(8,128)(2,1)} %wq.1, bf16[896,256]{1,0:T(8,128)(2,1)} %wk.1, bf16[896,256]{1,0:T(8,128)(2,1)} %wv.1, bf16[256,4096]{1,0:T(8,128)(2,1)} %wo.1, bf16[16,128,896]{2,1,0:T(8,128)(2,1)} %enc.1, ...), custom_call_target="tpu_custom_call" | custom-call | tf_op jit(solution)/shard_map/pallas_call | solution.py:521
  116.2 2.8 %add_convert_fusion = bf16[128,4096]{1,0:T(8,128)(2,1)} fusion(bf16[128,4096]{1,0:T(8,128)(2,1)} %get-tuple-element.8, bf16[128,4096]{1,0:T(8,128)(2,1)} %get-tuple-element.7), kind=kLoop, calls=%fused_computation | loop fusion | flops 2097152 | bytes 3145728 | tf_op jit(solution)/shard_map/convert_element_type | solution.py:577
